TPU v7x, 32 devices: a whole 2x2x4 slice. The times are simulated.
32 devices in a mesh: grp: 2 (over x), feat: 16 (over z, y, core).
Axes of the slice: x: 2, y: 2, z: 4, core: 2. Of those that a mesh axis runs over, the one named last changes fastest.
Arguments:
- node_feats: bfloat16 [65536, 128], P(('grp', 'feat')), parts along dimension 0, may hold values from -6 to 6
- tile_weights: bfloat16 [1024, 128, 128], P(('grp', 'feat')), parts along dimension 0, may hold values from 0 to 1
- source_slots: int32 [1024], P(('grp', 'feat')), parts along dimension 0, may hold values from 0 to 16, as said below
- target_slots: int32 [1024], P(('grp', 'feat')), parts along dimension 0, may hold values from 0 to 16, as said below
- self_weight: bfloat16 [128, 1024], replicated, may hold values from -0.5 to 0.5
- neigh_weight: bfloat16 [128, 1024], replicated, may hold values from -0.5 to 0.5
- hidden_bias: float32 [1024], replicated, may hold values from -3 to 3
- out_grad: bfloat16 [65536, 1024], P(('grp', 'feat')), parts along dimension 0, may hold values from -6 to 6
Outputs:
- feat_grad: bfloat16 [65536, 128], P(('grp', 'feat')), parts along dimension 0
- self_grad: float32 [256, 1024], P('grp', 'feat'), parts along dimension 0
- neigh_grad: float32 [256, 1024], P('grp', 'feat'), parts along dimension 0
- bias_grad: float32 [2048], P(('grp', 'feat')), parts along dimension 0
There are 2 independent parts, one for each index of `grp`. A program takes and returns all parts, laid end to end along the dimension named above; an argument that names none is the same for every part. Nothing has to cross between parts.
Inputs may be any that keep to these rules, and one draw needn't show every extreme that they name: `source_slots`: entry (s, r, k) is empty (16) exactly when target_slots entry (r, s, k) is empty. Filled slots of one pair of owners are uneven across owners; some owner receives 2 tiles from every owner. `target_slots`: empty entries (16) match those of source_slots as stated there.
All inputs are finite; a program needn't handle non-finite values.
Results may differ from a plain program's by a relative error of at most 0.0085.
The roundings to bfloat16 on the way count: a program that leaves them out, or rounds other values in their place, can miss the bound.
Values may be sent and summed in bfloat16 or wider, within the bound.
A program may use at most 128 MiB of HBM per device.

v0:
```python
import jax
import jax.numpy as jnp
from jax import lax
from jax.sharding import PartitionSpec as P

FEATS = 128
HIDDEN_SIZE = 1024
TILE = 128
CAPACITY = 2
NODE_DEV = 2048


def normalize(active):
    return active * lax.rsqrt(jnp.mean(active * active, axis=-1, keepdims=True) + 1e-05)


def local(
    node_feats,
    tile_weights,
    source_slots,
    target_slots,
    self_weight,
    neigh_weight,
    hidden_bias,
    out_grad,
):
    peers = lax.axis_size("feat")
    blocks_dev = NODE_DEV // TILE
    slot_total = peers * CAPACITY
    block_ids = jnp.arange(blocks_dev, dtype=jnp.int32)
    filled = source_slots < blocks_dev
    clipped = jnp.minimum(source_slots, blocks_dev - 1)
    local_blocks = node_feats.reshape(blocks_dev, TILE, FEATS)
    picked = jnp.where(filled[:, None, None], local_blocks[clipped], jnp.zeros((), jnp.bfloat16))
    products = jnp.einsum(
        "tij,tjc->tic", tile_weights, picked, preferred_element_type=jnp.float32
    ).astype(jnp.bfloat16)
    arrived = lax.all_to_all(
        products.reshape(peers, CAPACITY, TILE, FEATS),
        "feat",
        split_axis=0,
        concat_axis=0,
        tiled=True,
    )
    onehot = (target_slots[:, None] == block_ids[None, :]).astype(jnp.bfloat16)
    summed = lax.dot_general(
        onehot,
        arrived.reshape(slot_total, TILE * FEATS),
        (((0,), (0,)), ((), ())),
        preferred_element_type=jnp.float32,
    )
    neigh_mean = summed.astype(jnp.bfloat16).reshape(NODE_DEV, FEATS)
    preact = (
        jnp.dot(node_feats, self_weight, preferred_element_type=jnp.float32)
        + jnp.dot(neigh_mean, neigh_weight, preferred_element_type=jnp.float32)
        + hidden_bias
    )
    active = jnp.maximum(preact, 0.0)
    output_value, pullback = jax.vjp(normalize, active)
    active_grad = pullback(out_grad.astype(jnp.float32))[0]
    pre_grad = jnp.where(preact > 0.0, active_grad, 0.0).astype(jnp.bfloat16)
    bias_local = jnp.sum(pre_grad.astype(jnp.float32), axis=0)
    self_local = lax.dot_general(
        node_feats, pre_grad, (((0,), (0,)), ((), ())), preferred_element_type=jnp.float32
    )
    neigh_local = lax.dot_general(
        neigh_mean, pre_grad, (((0,), (0,)), ((), ())), preferred_element_type=jnp.float32
    )
    mean_grad = jnp.dot(pre_grad, neigh_weight.T, preferred_element_type=jnp.float32)
    mean_grad = mean_grad.astype(jnp.bfloat16).reshape(blocks_dev, TILE * FEATS)
    returned = jnp.dot(onehot, mean_grad, preferred_element_type=jnp.float32).astype(jnp.bfloat16)
    came_back = lax.all_to_all(
        returned.reshape(peers, CAPACITY, TILE, FEATS),
        "feat",
        split_axis=0,
        concat_axis=0,
        tiled=True,
    )
    spread = jnp.einsum(
        "tji,tjc->tic",
        tile_weights,
        came_back.reshape(slot_total, TILE, FEATS),
        preferred_element_type=jnp.float32,
    )
    source_hot = (source_slots[:, None] == block_ids[None, :]).astype(jnp.float32)
    gathered_back = lax.dot_general(
        source_hot,
        spread.reshape(slot_total, TILE * FEATS),
        (((0,), (0,)), ((), ())),
        precision=lax.Precision.HIGHEST,
        preferred_element_type=jnp.float32,
    )
    feat_grad = (
        jnp.dot(pre_grad, self_weight.T, preferred_element_type=jnp.float32)
        + gathered_back.reshape(NODE_DEV, FEATS)
    ).astype(jnp.bfloat16)
    self_sum, neigh_sum, bias_sum = lax.psum((self_local, neigh_local, bias_local), "feat")
    share_width = HIDDEN_SIZE // peers
    offset = lax.axis_index("feat") * share_width
    self_grad = lax.dynamic_slice_in_dim(self_sum, offset, share_width, 1)
    neigh_grad = lax.dynamic_slice_in_dim(neigh_sum, offset, share_width, 1)
    bias_grad = lax.dynamic_slice_in_dim(bias_sum, offset, share_width, 0)
    return (feat_grad, self_grad, neigh_grad, bias_grad)


def solution(mesh):
    in_specs = (
        P(("grp", "feat"), None),
        P(("grp", "feat"), None, None),
        P(("grp", "feat")),
        P(("grp", "feat")),
        P(),
        P(),
        P(),
        P(("grp", "feat"), None),
    )
    out_specs = (P(("grp", "feat"), None), P("grp", "feat"), P("grp", "feat"), P(("grp", "feat")))
    return jax.shard_map(local, mesh=mesh, in_specs=in_specs, out_specs=out_specs, check_vma=False)
```

profile of v0, /device:TPU:0, one launch (start us, length us, event | category | flops | bytes accessed | tf_op | source)
XLA Modules:
  0.0 191.7 jit_solution(7725591948679941953)
XLA Ops:
  7.2 0.0 copy-start
  7.2 0.7 compare_select_fusion
  7.9 0.7 broadcast_compare_fusion
  8.6 1.8 gather_fusion
  10.4 0.0 copy-done
  10.4 1.0 convolution_convert_fusion.3
  11.4 1.3 copy.15
  12.7 7.4 %all-to-all-start = ((bf16[16,2,128,128]{3,2,1,0:T(8,128)(2,1)}), bf16[16,2,128,128]{3,2,1,0:T(8,128)(2,1)S(1)}, u32[]{:S(2)}, u32[]{:S(2)}) async-start(bf16[16,2,128,128]{3,2,1,0:T(8,128)(2,1)} %copy.15), calls=%async_computation | async-start | bytes 2097152 | tf_op jit(solution)/shard_map/all_to_all | solution.py:38
  20.1 0.0 copy-start.4
  20.2 0.0 copy-start.6
  20.2 6.5 %copy.16 = bf16[2048,1024]{0,1:T(8,128)(2,1)} copy(bf16[2048,1024]{1,0:T(8,128)(2,1)} %param.15) | data formatting | bytes 8388608 | tf_op args[7]
  26.7 0.0 copy-done.4
  26.7 0.0 copy-done.6
  26.7 0.0 copy-start.8
  26.7 4.5 %fusion.19 = f32[2048,1024]{0,1:T(8,128)} fusion(bf16[2048,128]{1,0:T(8,128)(2,1)S(1)} %copy-done.4, bf16[128,1024]{1,0:T(8,128)(2,1)S(1)} %copy-done.6), kind=kOutput, calls=%fused_computation.41 | convolution fusion | flops 536870912 | bytes 9175040 | tf_op jit(solution)/shard_map/dot_general | solution.py:54
  31.3 11.8 %all-to-all-done = bf16[16,2,128,128]{3,2,1,0:T(8,128)(2,1)S(1)} async-done(((bf16[16,2,128,128]{3,2,1,0:T(8,128)(2,1)}), bf16[16,2,128,128]{3,2,1,0:T(8,128)(2,1)S(1)}, u32[]{:S(2)}, u32[]{:S(2)}) %all-to-all-start) | async-done | bytes 1048608 | tf_op jit(solution)/shard_map/all_to_all | solution.py:38
  43.1 0.0 copy-done.9
  43.1 0.7 convolution_convert_fusion.1
  43.8 0.2 reshape.58
  44.1 0.0 copy-done.8
  44.1 0.0 copy-start.3
  44.1 6.3 %multiply_reduce_fusion = (f32[2048]{0:T(1024)S(1)}, f32[2048]{0:T(1024)S(1)}, f32[2048,1024]{0,1:T(8,128)S(1)}) fusion(bf16[2048,1024]{0,1:T(8,128)(2,1)} %copy.16, f32[1024]{0:T(1024)S(1)} %copy-done.8, f32[2048,1024]{0,1:T(8,128)} %fusion.19, bf16[2048,128]{1,0:T(8,128)(2,1)S(1)} %reshape.58, bf16[128,1024]{1,0:T(8,128)(2,1)} %param.13), kind=kOutput, calls=%fused_computation.10 | convolution fusion | flops 553644032 | bytes 21778432 | tf_op jit(solution)/shard_map/dot_general | solution.py:55
  50.4 0.0 copy-done.3
  50.4 0.0 copy-start.7
  50.4 2.8 %convert_reduce_fusion = (f32[1024]{0:T(1024)S(1)}, bf16[2048,1024]{0,1:T(8,128)(2,1)S(1)}) fusion(f32[2048]{0:T(1024)S(1)} %get-tuple-element.11, f32[2048,1024]{0,1:T(8,128)S(1)} %get-tuple-element.12, f32[2048]{0:T(1024)S(1)} %get-tuple-element.10, bf16[2048,1024]{0,1:T(8,128)(2,1)S(1)} %copy-done.3), kind=kLoop, calls=%fused_computation.9 | loop fusion | flops 23067648 | bytes 16797696 | tf_op jit(solution)/shard_map/reduce_sum | solution.py:62
  53.2 0.0 copy-start.1
  53.2 1.9 %copy-done.1 = bf16[2048,1024]{0,1:T(8,128)(2,1)} copy-done((bf16[2048,1024]{0,1:T(8,128)(2,1)}, bf16[2048,1024]{0,1:T(8,128)(2,1)S(1)}, u32[]{:S(2)}) %copy-start.1) | copy-done | bytes 4194328
  55.1 0.0 copy-done.7
  55.1 1.3 convolution_convert_fusion.2
  56.5 0.2 reshape.59
  56.7 0.5 fusion.7
  57.2 1.2 copy.21
  58.4 6.9 %all-to-all-start.1 = ((bf16[16,2,128,128]{3,2,1,0:T(8,128)(2,1)}), bf16[16,2,128,128]{3,2,1,0:T(8,128)(2,1)S(1)}, u32[]{:S(2)}, u32[]{:S(2)}) async-start(bf16[16,2,128,128]{3,2,1,0:T(8,128)(2,1)} %bitcast.13), calls=%async_computation.1 | async-start | bytes 2097152 | tf_op jit(solution)/shard_map/all_to_all | solution.py:72
  65.2 0.0 all-reduce.3.cloned.1.call-start
  65.3 4.4 %fusion.20 = f32[128,1024]{0,1:T(8,128)} fusion(bf16[2048,1024]{0,1:T(8,128)(2,1)} %copy-done.1, bf16[2048,128]{1,0:T(8,128)(2,1)S(1)} %reshape.58), kind=kOutput, calls=%fused_computation.42 | convolution fusion | flops 536870912 | bytes 5242880 | tf_op jit(solution)/shard_map/dot_general | solution.py:66
  69.7 2.0 %convolution_bitcast_fusion.1 = f32[128,1024]{0,1:T(8,128)} fusion(bf16[2048,1024]{0,1:T(8,128)(2,1)S(1)} %copy-done.2, bf16[2048,128]{1,0:T(8,128)(2,1)S(1)} %copy-done.4), kind=kOutput, calls=%fused_computation.21 | convolution fusion | flops 536870912 | bytes 5242880 | tf_op jit(solution)/shard_map/dot_general | solution.py:63
  71.7 0.0 all-reduce.3.cloned.1.call-update
  71.8 40.7 %psum.23 = f32[1024]{0:T(1024)S(1)} all-reduce(f32[1024]{0:T(1024)S(1)} %get-tuple-element.8), channel_id=1, replica_groups=mesh['grp'=2,'feat'=16] {'feat'}, use_global_device_ids=true, to_apply=%region_5.6 | all-reduce | flops 1024 | bytes 8192 | tf_op jit(solution)/shard_map/psum | solution.py:97
  112.5 0.6 dynamic_slice.11
  113.1 57.8 %all-reduce.3.cloned.1.call-done = (f32[128,1024]{0,1:T(8,128)}, f32[128,1024]{0,1:T(8,128)}) async-done(((f32[128,1024]{0,1:T(8,128)}, f32[128,1024]{0,1:T(8,128)}), (f32[128,1024]{0,1:T(8,128)}, f32[128,1024]{0,1:T(8,128)})) %all-reduce.3.cloned.1.call-update) | async-done | bytes 1048592 | tf_op jit(solution)/shard_map/psum | solution.py:97
  170.9 1.4 constant_dynamic-slice_fusion
  172.3 0.0 all-to-all-done.1
  172.3 1.0 copy-done.5
  173.2 1.8 convolution_bitcast_fusion
  175.0 1.8 copy.18
  176.9 3.6 %fusion.4 = f32[16,16384]{1,0:T(8,128)S(1)} fusion(f32[4,8,128,128]{3,2,1,0:T(8,128)} %bitcast.40, s32[32]{0:T(128)S(1)} %copy-done.10), kind=kOutput, calls=%fused_computation.15 | convolution fusion | flops 100663808 | bytes 3145856 | tf_op jit(solution)/shard_map/dot_general | solution.py:86
  180.4 0.2 reshape.63
  180.6 4.3 %fusion.3 = bf16[2048,128]{1,0:T(8,128)(2,1)} fusion(f32[2048,128]{1,0:T(8,128)S(1)} %reshape.63, bf16[2048,1024]{0,1:T(8,128)(2,1)} %copy-done.1, bf16[128,1024]{1,0:T(8,128)(2,1)S(1)} %copy-done.6), kind=kOutput, calls=%fused_computation.13 | convolution fusion | flops 537395200 | bytes 6029312 | tf_op jit(solution)/shard_map/dot_general | solution.py:94
  (8 shorter events, 0.0 us)
Async XLA Ops:
  7.2 3.2 %copy-start = (bf16[32,128,128]{2,1,0:T(8,128)(2,1)S(1)}, bf16[32,128,128]{2,1,0:T(8,128)(2,1)}, u32[]{:S(2)}) copy-start(bf16[32,128,128]{2,1,0:T(8,128)(2,1)} %param.9) | copy-start | bytes 3145732
  12.7 30.3 %all-to-all-start = ((bf16[16,2,128,128]{3,2,1,0:T(8,128)(2,1)}), bf16[16,2,128,128]{3,2,1,0:T(8,128)(2,1)S(1)}, u32[]{:S(2)}, u32[]{:S(2)}) async-start(bf16[16,2,128,128]{3,2,1,0:T(8,128)(2,1)} %copy.15), calls=%async_computation | async-start | bytes 2097152 | tf_op jit(solution)/shard_map/all_to_all | solution.py:38
  20.1 6.6 %copy-start.4 = (bf16[2048,128]{1,0:T(8,128)(2,1)S(1)}, bf16[2048,128]{1,0:T(8,128)(2,1)}, u32[]{:S(2)}) copy-start(bf16[2048,128]{1,0:T(8,128)(2,1)} %param.8) | copy-start | bytes 1572868
  20.2 6.6 %copy-start.6 = (bf16[128,1024]{1,0:T(8,128)(2,1)S(1)}, bf16[128,1024]{1,0:T(8,128)(2,1)}, u32[]{:S(2)}) copy-start(bf16[128,1024]{1,0:T(8,128)(2,1)} %param.12) | copy-start | bytes 786436
  26.7 16.4 %copy-start.9 = (s32[32]{0:T(128)S(1)}, s32[32]{0:T(128)}, u32[]{:S(2)}) copy-start(s32[32]{0:T(128)} %param.11) | copy-start | bytes 388
  26.7 17.3 %copy-start.8 = (f32[1024]{0:T(1024)S(1)}, f32[1024]{0:T(1024)}, u32[]{:S(2)}) copy-start(f32[1024]{0:T(1024)} %param.14) | copy-start | bytes 12292
  44.1 6.3 %copy-start.3 = (bf16[2048,1024]{0,1:T(8,128)(2,1)S(1)}, bf16[2048,1024]{0,1:T(8,128)(2,1)}, u32[]{:S(2)}) copy-start(bf16[2048,1024]{0,1:T(8,128)(2,1)} %copy.16) | copy-start | bytes 12582916
  50.4 4.7 %copy-start.7 = (bf16[128,1024]{1,0:T(8,128)(2,1)S(1)}, bf16[128,1024]{1,0:T(8,128)(2,1)}, u32[]{:S(2)}) copy-start(bf16[128,1024]{1,0:T(8,128)(2,1)} %param.13) | copy-start | bytes 786436
  53.2 1.9 %copy-start.1 = (bf16[2048,1024]{0,1:T(8,128)(2,1)}, bf16[2048,1024]{0,1:T(8,128)(2,1)S(1)}, u32[]{:S(2)}) copy-start(bf16[2048,1024]{0,1:T(8,128)(2,1)S(1)} %get-tuple-element.9) | copy-start | bytes 12582916
  58.4 113.9 %all-to-all-start.1 = ((bf16[16,2,128,128]{3,2,1,0:T(8,128)(2,1)}), bf16[16,2,128,128]{3,2,1,0:T(8,128)(2,1)S(1)}, u32[]{:S(2)}, u32[]{:S(2)}) async-start(bf16[16,2,128,128]{3,2,1,0:T(8,128)(2,1)} %bitcast.13), calls=%async_computation.1 | async-start | bytes 2097152 | tf_op jit(solution)/shard_map/all_to_all | solution.py:72
  65.2 105.6 %all-reduce.3.cloned.1.call-start = ((), (), s32[]{:S(2)}) async-start(), calls=%async_computation.2 | async-start | bytes 2097152 | tf_op jit(solution)/shard_map/psum | solution.py:97
  65.3 4.4 %copy-start.2 = (bf16[2048,1024]{0,1:T(8,128)(2,1)S(1)}, bf16[2048,1024]{0,1:T(8,128)(2,1)}, u32[]{:S(2)}) copy-start(bf16[2048,1024]{0,1:T(8,128)(2,1)} %copy-done.1) | copy-start | bytes 12582916
  172.3 1.0 copy-start.5
  173.2 3.6 %copy-start.10 = (s32[32]{0:T(128)S(1)}, s32[32]{0:T(128)}, u32[]{:S(2)}) copy-start(s32[32]{0:T(128)} %param.10) | copy-start | bytes 388
Sparse Core Ops, SparseCore 0:
  71.9 98.9 all-reduce.2
where the time goes:
time: 192 us
  waiting for transfers between devices  69.6 us (36%)
  blocking collectives  40.7 us (21%)
  matrix products  30.3 us (16%)
  local copies, waits for them, and re-layouts  18.3 us (10%)
  starting transfers between devices  14.3 us (7%)
  between operations  14.2 us (7%)
  other arithmetic  4.19 us (2%)
    psum x1, waiting for transfers between devices, local(): lax.psum((self_local, neigh_local, bias_local), 'feat')  57.8 us
    psum x1, blocking collectives, local(): lax.psum((self_local, neigh_local, bias_local), 'feat')  40.7 us
    all_to_all x1, waiting for transfers between devices, local(): lax.all_to_all(products.reshape(peers, CAPACITY, TILE, FEATS), 'feat', sp...  11.8 us
    unnamed x24, local copies, waits for them, and re-layouts  10.7 us
    all_to_all x1, starting transfers between devices, local(): lax.all_to_all(products.reshape(peers, CAPACITY, TILE, FEATS), 'feat', sp...  7.39 us
    all_to_all x1, starting transfers between devices, local(): lax.all_to_all(returned.reshape(peers, CAPACITY, TILE, FEATS), 'feat', sp...  6.86 us
    dot_general x1, matrix products, local(): jnp.dot(neigh_mean, neigh_weight, preferred_element_type=jnp.float32)  6.26 us
    dot_general x1, matrix products, local(): jnp.dot(node_feats, self_weight, preferred_element_type=jnp.float32)  4.52 us
  transfers between devices with their start and end apart: 3, of which 2 were waited for; matrix products, arithmetic and copies ran while one was open for 10% of the time, Pallas kernels for 0%

commit v1 on v0

v1 whole, which is shorter than its diff:
```python
import functools

import jax
import jax.numpy as jnp
from jax import lax
from jax.experimental import pallas as pl
from jax.experimental.pallas import tpu as pltpu
from jax.sharding import PartitionSpec as P

FEATS = 128
HIDDEN_SIZE = 1024
TILE = 128
CAPACITY = 2
NODE_DEV = 2048
BLOCKS = NODE_DEV // TILE
ROWS = 256
COLS = 256
BIAS_ROWS = 16
EARLY = 3
MESH = pl.DeviceIdType.MESH
F32 = jnp.float32
BF16 = jnp.bfloat16


def distance(step, n):
    q = jnp.maximum(step - 1, 0)
    far = n // 2 + ((q + 1) // 2) * (1 - 2 * (q % 2))
    return far * jnp.minimum(step, 1)


def split_bias(total):
    high = total.astype(BF16)
    low = (total - high.astype(F32)).astype(BF16)
    row = lax.broadcasted_iota(jnp.int32, (BIAS_ROWS, total.shape[1]), 0)
    both = jnp.where(row == 0, high.astype(F32), jnp.where(row == 1, low.astype(F32), 0.0))
    return both.astype(BF16)


def kernel(
    n,
    feats,
    tiles,
    source,
    target,
    self_w,
    neigh_w,
    bias,
    grad_hbm,
    feat_out,
    self_out,
    neigh_out,
    bias_out,
    grad,
    stage,
    arrived,
    back_stage,
    back,
    chain,
    weights,
    inputs,
    active,
    pre_grad,
    mean_grad,
    feat_self,
    weight_sum,
    bias_sum,
    pair_send,
    pair_recv,
    share_send,
    share_recv,
    swap_send,
    swap_recv,
    prev_t,
    last_t,
    prev_s,
    last_s,
    grad_sem,
    send_1,
    recv_1,
    send_2,
    recv_2,
    pair_sems,
    send_b,
    recv_b,
    swap_sems,
):
    chips = n // 2
    width = 2 * HIDDEN_SIZE // n
    half = width // 2
    slots = n * CAPACITY
    me = lax.axis_index("feat")
    core = me % 2
    chip = me // 2
    sibling = chip * 2 + 1 - core

    barrier = pltpu.get_barrier_semaphore()

    @pl.loop(1, n)
    def _(d):
        pl.semaphore_signal(
            barrier, inc=1, device_id={"feat": (me + d) % n}, device_id_type=MESH
        )

    grad_copy = pltpu.make_async_copy(grad_hbm, grad, grad_sem)
    grad_copy.start()

    def product(slot):
        block = feats[jnp.minimum(source[slot], BLOCKS - 1)]
        return jnp.dot(tiles[slot], block, preferred_element_type=F32).astype(BF16)

    def forward_copy(step):
        to = (me + distance(step, n)) % n
        return pltpu.make_async_remote_copy(
            src_ref=stage.at[to],
            dst_ref=arrived.at[me],
            send_sem=send_1.at[to],
            recv_sem=recv_1.at[me],
            device_id={"feat": to},
            device_id_type=MESH,
        )

    def forward_products(step):
        to = (me + distance(step, n)) % n
        for k in range(CAPACITY):
            stage[to, k] = product(to * CAPACITY + k)

    @pl.loop(1, 1 + EARLY)
    def _(step):
        forward_products(step)

    pl.semaphore_wait(barrier, n - 1)

    @pl.loop(1, 1 + EARLY)
    def _(step):
        forward_copy(step).start()

    @pl.loop(1 + EARLY, n)
    def _(step):
        forward_products(step)
        forward_copy(step).start()

    for k in range(CAPACITY):
        arrived[me, k] = product(me * CAPACITY + k)
    weights[:FEATS] = self_w[...]
    weights[FEATS:] = neigh_w[...]
    for b in range(BLOCKS):
        inputs[b * TILE : (b + 1) * TILE, :FEATS] = feats[b]
    chain[slots] = jnp.zeros((TILE, FEATS), F32)
    bias_sum[...] = jnp.zeros_like(bias_sum)

    for prev, last, table in ((prev_t, last_t, target), (prev_s, last_s, source)):
        for b in range(BLOCKS + 1):
            last[b] = slots

        @pl.loop(0, n)
        def _(step):
            owner = (me - distance(step, n) + n) % n
            for k in range(CAPACITY):
                at = step * CAPACITY + k
                block = table[owner * CAPACITY + k]
                prev[at] = last[block]
                for b in range(BLOCKS + 1):
                    last[b] = jnp.where(block == b, at, last[b])

    def forward_link(step, owner):
        for k in range(CAPACITY):
            at = step * CAPACITY + k
            chain[at] = arrived[owner, k].astype(F32) + chain[prev_t[at]]

    forward_link(0, me)

    @pl.loop(1, n)
    def _(step):
        owner = (me - distance(step, n) + n) % n
        pltpu.make_async_remote_copy(
            src_ref=stage.at[owner],
            dst_ref=arrived.at[owner],
            send_sem=send_1.at[owner],
            recv_sem=recv_1.at[owner],
            device_id={"feat": owner},
            device_id_type=MESH,
        ).wait_recv()
        forward_link(step, owner)

    for b in range(BLOCKS):
        inputs[b * TILE : (b + 1) * TILE, FEATS:] = chain[last_t[b]].astype(BF16)
    grad_copy.wait()

    @pl.loop(0, NODE_DEV // ROWS)
    def _(part):
        rows = pl.ds(pl.multiple_of(part * ROWS, ROWS), ROWS)
        x = inputs[rows, :]
        squares = jnp.zeros((ROWS, 128), F32)
        crosses = jnp.zeros((ROWS, 128), F32)
        for c in range(0, HIDDEN_SIZE, COLS):
            cols = slice(c, c + COLS)
            pre = jnp.dot(x, weights[:, cols], preferred_element_type=F32) + bias[:, cols]
            a = jnp.maximum(pre, 0.0)
            active[:, cols] = a
            g = grad[rows, cols].astype(F32)
            aa = a * a
            ag = a * g
            for e in range(0, COLS, 128):
                squares += aa[:, e : e + 128]
                crosses += ag[:, e : e + 128]
        scale = lax.rsqrt(jnp.sum(squares, axis=1, keepdims=True) / HIDDEN_SIZE + 1e-05)
        pull = scale * scale * scale * (jnp.sum(crosses, axis=1, keepdims=True) / HIDDEN_SIZE)
        for c in range(0, HIDDEN_SIZE, COLS):
            cols = slice(c, c + COLS)
            a = active[:, cols]
            g = grad[rows, cols].astype(F32)
            p = jnp.where(a > 0.0, scale * g - pull * a, 0.0).astype(BF16)
            pre_grad[rows, cols] = p
            bias_sum[:, cols] += jnp.sum(p.astype(F32).reshape(ROWS // 8, 8, COLS), axis=0)
        both = lax.dot_general(
            pre_grad[rows, :],
            weights[...],
            (((1,), (1,)), ((), ())),
            preferred_element_type=F32,
        )
        for e in range(ROWS // TILE):
            b = part * (ROWS // TILE) + e
            feat_self[b] = both[e * TILE : (e + 1) * TILE, :FEATS]
            mean_grad[b] = both[e * TILE : (e + 1) * TILE, FEATS:].astype(BF16)

    def backward_copy(step):
        to = (me + distance(step, n)) % n
        return pltpu.make_async_remote_copy(
            src_ref=back_stage.at[to],
            dst_ref=back.at[me],
            send_sem=send_2.at[to],
            recv_sem=recv_2.at[me],
            device_id={"feat": to},
            device_id_type=MESH,
        )

    def backward_send(step):
        to = (me + distance(step, n)) % n
        for k in range(CAPACITY):
            block = jnp.minimum(target[to * CAPACITY + k], BLOCKS - 1)
            back_stage[to, k] = mean_grad[block]
        backward_copy(step).start()

    @pl.loop(1, 1 + n // 2)
    def _(step):
        backward_send(step)

    for c in range(0, HIDDEN_SIZE, COLS):
        cols = slice(c, c + COLS)
        local = lax.dot_general(
            inputs[...],
            pre_grad[:, cols],
            (((0,), (0,)), ((), ())),
            preferred_element_type=F32,
        )
        weight_sum[0, :, cols] = local[:FEATS]
        weight_sum[1, :, cols] = local[FEATS:]
    bias_row = jnp.sum(bias_sum[...], axis=0, keepdims=True)
    for c in range(chips):
        cols = slice(c * width, (c + 1) * width)
        pair_send[c, :FEATS] = weight_sum[1 - core, :, cols].astype(BF16)
        pair_send[c, FEATS:] = split_bias(bias_row[:, cols])
    pair_copy = pltpu.make_async_remote_copy(
        src_ref=pair_send,
        dst_ref=pair_recv,
        send_sem=pair_sems.at[0],
        recv_sem=pair_sems.at[1],
        device_id={"feat": sibling},
        device_id_type=MESH,
    )
    pair_copy.start()
    pair_copy.wait_recv()
    for c in range(chips):
        cols = slice(c * width, (c + 1) * width)
        share_send[c, :FEATS] = (
            weight_sum[core, :, cols] + pair_recv[c, :FEATS].astype(F32)
        ).astype(BF16)
        other = jnp.sum(pair_recv[c, FEATS:].astype(F32), axis=0, keepdims=True)
        share_send[c, FEATS:] = split_bias(bias_row[:, cols] + other)

    def share_copy(to, slot):
        return pltpu.make_async_remote_copy(
            src_ref=share_send.at[to],
            dst_ref=share_recv.at[slot],
            send_sem=send_b.at[to],
            recv_sem=recv_b.at[slot],
            device_id={"feat": to * 2 + core},
            device_id_type=MESH,
        )

    @pl.loop(1, chips)
    def _(d):
        share_copy((chip + d) % chips, chip).start()

    @pl.loop(1 + n // 2, n)
    def _(step):
        backward_send(step)

    def backward_link(step, owner, blocks):
        for k in range(CAPACITY):
            at = step * CAPACITY + k
            spread = lax.dot_general(
                tiles[owner * CAPACITY + k],
                blocks[k],
                (((0,), (0,)), ((), ())),
                preferred_element_type=F32,
            )
            chain[at] = spread + chain[prev_s[at]]

    backward_link(
        0,
        me,
        [
            mean_grad[jnp.minimum(target[me * CAPACITY + k], BLOCKS - 1)]
            for k in range(CAPACITY)
        ],
    )

    def backward_take(step):
        owner = (me - distance(step, n) + n) % n
        pltpu.make_async_remote_copy(
            src_ref=back_stage.at[owner],
            dst_ref=back.at[owner],
            send_sem=send_2.at[owner],
            recv_sem=recv_2.at[owner],
            device_id={"feat": owner},
            device_id_type=MESH,
        ).wait_recv()
        backward_link(step, owner, [back[owner, k] for k in range(CAPACITY)])

    @pl.loop(1, 1 + n // 2)
    def _(step):
        backward_take(step)

    swap_send[...] = share_send[chip].astype(F32)

    @pl.loop(1, chips)
    def _(d):
        other = (chip + d) % chips
        share_copy(other, other).wait_recv()
        swap_send[...] += share_recv[other].astype(F32)

    swap_copy = pltpu.make_async_remote_copy(
        src_ref=swap_send,
        dst_ref=swap_recv,
        send_sem=swap_sems.at[0],
        recv_sem=swap_sems.at[1],
        device_id={"feat": sibling},
        device_id_type=MESH,
    )
    swap_copy.start()

    @pl.loop(1 + n // 2, n)
    def _(step):
        backward_take(step)

    for b in range(BLOCKS):
        feat_out[b] = (feat_self[b] + chain[last_s[b]]).astype(BF16)

    swap_copy.wait_recv()

    def own_half(block):
        return jnp.where(core == 0, block[:, :half], block[:, half:])

    mine = own_half(swap_send[:FEATS])
    theirs = own_half(swap_recv[:FEATS])
    self_out[...] = jnp.where(core == 0, mine, theirs)
    neigh_out[...] = jnp.where(core == 0, theirs, mine)
    bias_out[...] = own_half(jnp.sum(swap_send[FEATS:], axis=0, keepdims=True))

    swap_copy.wait_send()
    pair_copy.wait_send()

    @pl.loop(1, chips)
    def _(d):
        share_copy((chip + d) % chips, chip).wait_send()

    @pl.loop(1, n)
    def _(step):
        forward_copy(step).wait_send()
        backward_copy(step).wait_send()


def local(
    node_feats,
    tile_weights,
    source_slots,
    target_slots,
    self_weight,
    neigh_weight,
    hidden_bias,
    out_grad,
):
    n = lax.axis_size("feat")
    slots = n * CAPACITY
    chips = n // 2
    width = 2 * HIDDEN_SIZE // n
    share_rows = FEATS + BIAS_ROWS
    vmem = pl.BlockSpec(memory_space=pltpu.VMEM)
    smem = pl.BlockSpec(memory_space=pltpu.SMEM)
    dma = pltpu.SemaphoreType.DMA
    block = (TILE, FEATS)
    flops = 2 * NODE_DEV * HIDDEN_SIZE * FEATS * 6 + 4 * slots * TILE * TILE * FEATS
    feat_grad, self_grad, neigh_grad, bias_grad = pl.pallas_call(
        functools.partial(kernel, n),
        out_shape=(
            jax.ShapeDtypeStruct((BLOCKS,) + block, BF16),
            jax.ShapeDtypeStruct((FEATS, width // 2), F32),
            jax.ShapeDtypeStruct((FEATS, width // 2), F32),
            jax.ShapeDtypeStruct((1, width // 2), F32),
        ),
        in_specs=[vmem, vmem, smem, smem, vmem, vmem, vmem, pl.BlockSpec(memory_space=pl.ANY)],
        out_specs=(vmem, vmem, vmem, vmem),
        scratch_shapes=[
            pltpu.VMEM((NODE_DEV, HIDDEN_SIZE), BF16),
            pltpu.VMEM((n, CAPACITY) + block, BF16),
            pltpu.VMEM((n, CAPACITY) + block, BF16),
            pltpu.VMEM((n, CAPACITY) + block, BF16),
            pltpu.VMEM((n, CAPACITY) + block, BF16),
            pltpu.VMEM((slots + 1,) + block, F32),
            pltpu.VMEM((2 * FEATS, HIDDEN_SIZE), BF16),
            pltpu.VMEM((NODE_DEV, 2 * FEATS), BF16),
            pltpu.VMEM((ROWS, HIDDEN_SIZE), F32),
            pltpu.VMEM((NODE_DEV, HIDDEN_SIZE), BF16),
            pltpu.VMEM((BLOCKS,) + block, BF16),
            pltpu.VMEM((BLOCKS,) + block, F32),
            pltpu.VMEM((2, FEATS, HIDDEN_SIZE), F32),
            pltpu.VMEM((8, HIDDEN_SIZE), F32),
            pltpu.VMEM((chips, share_rows, width), BF16),
            pltpu.VMEM((chips, share_rows, width), BF16),
            pltpu.VMEM((chips, share_rows, width), BF16),
            pltpu.VMEM((chips, share_rows, width), BF16),
            pltpu.VMEM((share_rows, width), F32),
            pltpu.VMEM((share_rows, width), F32),
            pltpu.SMEM((slots,), jnp.int32),
            pltpu.SMEM((BLOCKS + 1,), jnp.int32),
            pltpu.SMEM((slots,), jnp.int32),
            pltpu.SMEM((BLOCKS + 1,), jnp.int32),
            dma,
            dma((n,)),
            dma((n,)),
            dma((n,)),
            dma((n,)),
            dma((2,)),
            dma((chips,)),
            dma((chips,)),
            dma((2,)),
        ],
        compiler_params=pltpu.CompilerParams(
            collective_id=0, has_side_effects=True, vmem_limit_bytes=56 * 2**20
        ),
        cost_estimate=pl.CostEstimate(flops=flops, bytes_accessed=8 * 2**20, transcendentals=0),
    )(
        node_feats.reshape((BLOCKS,) + block),
        tile_weights,
        source_slots,
        target_slots,
        self_weight,
        neigh_weight,
        hidden_bias.reshape(1, HIDDEN_SIZE),
        out_grad,
    )
    return (
        feat_grad.reshape(NODE_DEV, FEATS),
        self_grad,
        neigh_grad,
        bias_grad.reshape(width // 2),
    )


def solution(mesh):
    in_specs = (
        P(("grp", "feat"), None),
        P(("grp", "feat"), None, None),
        P(("grp", "feat")),
        P(("grp", "feat")),
        P(),
        P(),
        P(),
        P(("grp", "feat"), None),
    )
    out_specs = (P(("grp", "feat"), None), P("grp", "feat"), P("grp", "feat"), P(("grp", "feat")))
    return jax.shard_map(local, mesh=mesh, in_specs=in_specs, out_specs=out_specs, check_vma=False)
```

time: 192 us -> 75.9 us (0.40)
  waiting for transfers between devices: 69.6 us -> 0 us
  Pallas kernels: 0 us -> 68.9 us
  blocking collectives: 40.7 us -> 0 us
  matrix products: 30.3 us -> 0 us
  starting transfers between devices: 14.3 us -> 0 us
  between operations: 14.2 us -> 0.64 us
  local copies, waits for them, and re-layouts: 18.3 us -> 6.11 us
  other arithmetic: 4.19 us -> 0 us
    pallas_call x0 -> x1, Pallas kernels: none -> 68.9 us  [local(): pl.pallas_call(functools.partial(kernel, n), out_shape=(jax.ShapeDtypeStr...]
    psum x1 -> x0, waiting for transfers between devices: 57.8 us -> none  [local(): lax.psum((self_local, neigh_local, bias_local), 'feat')]
    psum x1 -> x0, blocking collectives: 40.7 us -> none  [local(): lax.psum((self_local, neigh_local, bias_local), 'feat')]
    dot_general x11 -> x0, matrix products: 30.3 us -> none  [the longest x1 6.26 us: local(): jnp.dot(neigh_mean, neigh_weight, preferred_element_type=jnp.float32)]
    all_to_all x2 -> x0, starting transfers between devices: 14.3 us -> none  [the longest x1 7.39 us: local(): lax.all_to_all(products.reshape(peers, CAPACITY, TILE, FEATS), 'feat', sp...]
    all_to_all x2 -> x0, waiting for transfers between devices: 11.8 us -> none  [the longest x1 11.8 us: local(): lax.all_to_all(products.reshape(peers, CAPACITY, TILE, FEATS), 'feat', sp...]
    unnamed x24 -> x4, local copies, waits for them, and re-layouts: 10.7 us -> 6.11 us
    reduce_sum x1 -> x0, other arithmetic: 2.76 us -> none  [local(): bias_local = jnp.sum(pre_grad.astype(jnp.float32), axis=0)]
  transfers between devices with their start and end apart: 3 -> 0, of which waited for: 2 -> 0; matrix products, arithmetic and copies ran while one was open for 10% -> 0% of each run, Pallas kernels for 0% -> 0%
where the time goes in v1:
time: 75.9 us; the launch traced here: 75.7 us
  Pallas kernels  68.9 us (91%)
  local copies, waits for them, and re-layouts  6.11 us (8%)
    pallas_call x1, Pallas kernels, local(): pl.pallas_call(functools.partial(kernel, n), out_shape=(jax.ShapeDtypeStr...  68.9 us
    unnamed x4, local copies, waits for them, and re-layouts  6.11 us

profile of v1, /device:TPU:0, one launch (start us, length us, event | category | flops | bytes accessed | tf_op | source)
XLA Modules:
  0.0 75.7 jit_solution(18049508867864771906)
XLA Ops:
  0.6 68.9 %shard_map.111 = (bf16[16,128,128]{2,1,0:T(8,128)(2,1)}, f32[128,64]{1,0:T(8,128)}, f32[128,64]{1,0:T(8,128)}, f32[1,64]{1,0:T(1,128)}) custom-call(bf16[16,128,128]{2,1,0:T(8,128)(2,1)} %bitcast.5, bf16[32,128,128]{2,1,0:T(8,128)(2,1)} %tiles.1, s32[32]{0:T(128)} %source.1, s32[32]{0:T(128)} %target.1, bf16[128,1024]{1,0:T(8,128)(2,1)} %self_w.1, ...), custom_call_target="tpu_custom_call" | custom-call | flops 3489660928 | bytes 8388608 | tf_op jit(solution)/shard_map/pallas_call | solution.py:404
  69.5 1.5 %copy.12 = f32[128,64]{0,1:T(8,128)} copy(f32[128,64]{1,0:T(8,128)} %get-tuple-element.13) | data formatting | bytes 65536
  71.1 1.5 %copy.13 = f32[128,64]{0,1:T(8,128)} copy(f32[128,64]{1,0:T(8,128)} %get-tuple-element.14) | data formatting | bytes 65536
  72.6 1.9 %copy.16 = bf16[2048,128]{1,0:T(8,128)(2,1)} copy(bf16[2048,128]{1,0:T(8,128)(2,1)} %bitcast.4) | data formatting | bytes 1048576
  74.5 1.2 %copy.17 = f32[64]{0:T(128)} copy(f32[64]{0:T(128)} %bitcast.7) | data formatting | bytes 512

commit v2 on v1

--- a/solution.py
+++ b/solution.py
@@ -17,6 +17,9 @@
 COLS = 256
 BIAS_ROWS = 16
 EARLY = 3
+PARTS = 2
+SLAB = TILE // PARTS
+PART_ROWS = NODE_DEV // PARTS
 MESH = pl.DeviceIdType.MESH
 F32 = jnp.float32
 BF16 = jnp.bfloat16
@@ -101,20 +104,26 @@
             barrier, inc=1, device_id={"feat": (me + d) % n}, device_id_type=MESH
         )
 
-    grad_copy = pltpu.make_async_copy(grad_hbm, grad, grad_sem)
-    grad_copy.start()
+    grad_copies = [
+        pltpu.make_async_copy(grad_hbm.at[:, h], grad.at[h], grad_sem.at[h]) for h in range(PARTS)
+    ]
+    for copy in grad_copies:
+        copy.start()
+
+    def slab(h):
+        return slice(h * SLAB, (h + 1) * SLAB)
 
     def product(slot):
         block = feats[jnp.minimum(source[slot], BLOCKS - 1)]
         return jnp.dot(tiles[slot], block, preferred_element_type=F32).astype(BF16)
 
-    def forward_copy(step):
+    def forward_copy(step, h):
         to = (me + distance(step, n)) % n
         return pltpu.make_async_remote_copy(
-            src_ref=stage.at[to],
-            dst_ref=arrived.at[me],
-            send_sem=send_1.at[to],
-            recv_sem=recv_1.at[me],
+            src_ref=stage.at[to, :, slab(h)],
+            dst_ref=arrived.at[me, :, slab(h)],
+            send_sem=send_1.at[h, to],
+            recv_sem=recv_1.at[h, me],
             device_id={"feat": to},
             device_id_type=MESH,
         )
@@ -132,19 +141,30 @@
 
     @pl.loop(1, 1 + EARLY)
     def _(step):
-        forward_copy(step).start()
+        forward_copy(step, 0).start()
 
     @pl.loop(1 + EARLY, n)
     def _(step):
         forward_products(step)
-        forward_copy(step).start()
+        forward_copy(step, 0).start()
+
+    for h in range(1, PARTS):
+
+        @pl.loop(1, n)
+        def _(step):
+            forward_copy(step, h).start()
+
+    def rows_of(h, b):
+        start = h * PART_ROWS + b * SLAB
+        return slice(start, start + SLAB)
 
     for k in range(CAPACITY):
         arrived[me, k] = product(me * CAPACITY + k)
     weights[:FEATS] = self_w[...]
     weights[FEATS:] = neigh_w[...]
-    for b in range(BLOCKS):
-        inputs[b * TILE : (b + 1) * TILE, :FEATS] = feats[b]
+    for h in range(PARTS):
+        for b in range(BLOCKS):
+            inputs[rows_of(h, b), :FEATS] = feats[b, slab(h)]
     chain[slots] = jnp.zeros((TILE, FEATS), F32)
     bias_sum[...] = jnp.zeros_like(bias_sum)
 
@@ -162,99 +182,117 @@
                 for b in range(BLOCKS + 1):
                     last[b] = jnp.where(block == b, at, last[b])
 
-    def forward_link(step, owner):
+    def forward_link(h, step, owner):
         for k in range(CAPACITY):
             at = step * CAPACITY + k
-            chain[at] = arrived[owner, k].astype(F32) + chain[prev_t[at]]
-
-    forward_link(0, me)
-
-    @pl.loop(1, n)
-    def _(step):
-        owner = (me - distance(step, n) + n) % n
-        pltpu.make_async_remote_copy(
-            src_ref=stage.at[owner],
-            dst_ref=arrived.at[owner],
-            send_sem=send_1.at[owner],
-            recv_sem=recv_1.at[owner],
-            device_id={"feat": owner},
-            device_id_type=MESH,
-        ).wait_recv()
-        forward_link(step, owner)
-
-    for b in range(BLOCKS):
-        inputs[b * TILE : (b + 1) * TILE, FEATS:] = chain[last_t[b]].astype(BF16)
-    grad_copy.wait()
-
-    @pl.loop(0, NODE_DEV // ROWS)
-    def _(part):
-        rows = pl.ds(pl.multiple_of(part * ROWS, ROWS), ROWS)
-        x = inputs[rows, :]
-        squares = jnp.zeros((ROWS, 128), F32)
-        crosses = jnp.zeros((ROWS, 128), F32)
-        for c in range(0, HIDDEN_SIZE, COLS):
-            cols = slice(c, c + COLS)
-            pre = jnp.dot(x, weights[:, cols], preferred_element_type=F32) + bias[:, cols]
-            a = jnp.maximum(pre, 0.0)
-            active[:, cols] = a
-            g = grad[rows, cols].astype(F32)
-            aa = a * a
-            ag = a * g
-            for e in range(0, COLS, 128):
-                squares += aa[:, e : e + 128]
-                crosses += ag[:, e : e + 128]
-        scale = lax.rsqrt(jnp.sum(squares, axis=1, keepdims=True) / HIDDEN_SIZE + 1e-05)
-        pull = scale * scale * scale * (jnp.sum(crosses, axis=1, keepdims=True) / HIDDEN_SIZE)
-        for c in range(0, HIDDEN_SIZE, COLS):
-            cols = slice(c, c + COLS)
-            a = active[:, cols]
-            g = grad[rows, cols].astype(F32)
-            p = jnp.where(a > 0.0, scale * g - pull * a, 0.0).astype(BF16)
-            pre_grad[rows, cols] = p
-            bias_sum[:, cols] += jnp.sum(p.astype(F32).reshape(ROWS // 8, 8, COLS), axis=0)
-        both = lax.dot_general(
-            pre_grad[rows, :],
-            weights[...],
-            (((1,), (1,)), ((), ())),
-            preferred_element_type=F32,
-        )
-        for e in range(ROWS // TILE):
-            b = part * (ROWS // TILE) + e
-            feat_self[b] = both[e * TILE : (e + 1) * TILE, :FEATS]
-            mean_grad[b] = both[e * TILE : (e + 1) * TILE, FEATS:].astype(BF16)
-
-    def backward_copy(step):
+            chain[at, slab(h)] = arrived[owner, k, slab(h)].astype(F32) + chain[prev_t[at], slab(h)]
+
+    def take_forward(h):
+        forward_link(h, 0, me)
+
+        @pl.loop(1, n)
+        def _(step):
+            owner = (me - distance(step, n) + n) % n
+            pltpu.make_async_remote_copy(
+                src_ref=stage.at[owner, :, slab(h)],
+                dst_ref=arrived.at[owner, :, slab(h)],
+                send_sem=send_1.at[h, owner],
+                recv_sem=recv_1.at[h, owner],
+                device_id={"feat": owner},
+                device_id_type=MESH,
+            ).wait_recv()
+            forward_link(h, step, owner)
+
+        for b in range(BLOCKS):
+            inputs[rows_of(h, b), FEATS:] = chain[last_t[b], slab(h)].astype(BF16)
+
+    def layer(h):
+        grad_copies[h].wait()
+        group = ROWS // SLAB
+
+        @pl.loop(0, PART_ROWS // ROWS)
+        def _(part):
+            rows = pl.ds(pl.multiple_of(h * PART_ROWS + part * ROWS, ROWS), ROWS)
+            blocks = pl.ds(part * group, group)
+            x = inputs[rows, :]
+            squares = jnp.zeros((ROWS, 128), F32)
+            crosses = jnp.zeros((ROWS, 128), F32)
+            for c in range(0, HIDDEN_SIZE, COLS):
+                cols = slice(c, c + COLS)
+                pre = jnp.dot(x, weights[:, cols], preferred_element_type=F32) + bias[:, cols]
+                a = jnp.maximum(pre, 0.0)
+                active[:, cols] = a
+                g = grad[h, blocks, :, cols].reshape(ROWS, COLS).astype(F32)
+                aa = a * a
+                ag = a * g
+                for e in range(0, COLS, 128):
+                    squares += aa[:, e : e + 128]
+                    crosses += ag[:, e : e + 128]
+            scale = lax.rsqrt(jnp.sum(squares, axis=1, keepdims=True) / HIDDEN_SIZE + 1e-05)
+            pull = scale * scale * scale * (jnp.sum(crosses, axis=1, keepdims=True) / HIDDEN_SIZE)
+            for c in range(0, HIDDEN_SIZE, COLS):
+                cols = slice(c, c + COLS)
+                a = active[:, cols]
+                g = grad[h, blocks, :, cols].reshape(ROWS, COLS).astype(F32)
+                p = jnp.where(a > 0.0, scale * g - pull * a, 0.0).astype(BF16)
+                pre_grad[rows, cols] = p
+                bias_sum[:, cols] += jnp.sum(p.astype(F32).reshape(ROWS // 8, 8, COLS), axis=0)
+            both = lax.dot_general(
+                pre_grad[rows, :],
+                weights[...],
+                (((1,), (1,)), ((), ())),
+                preferred_element_type=F32,
+            )
+            for e in range(group):
+                b = part * group + e
+                feat_self[b, slab(h)] = both[e * SLAB : (e + 1) * SLAB, :FEATS]
+                mean_grad[b, slab(h)] = both[e * SLAB : (e + 1) * SLAB, FEATS:].astype(BF16)
+
+    def backward_copy(step, h):
         to = (me + distance(step, n)) % n
         return pltpu.make_async_remote_copy(
-            src_ref=back_stage.at[to],
-            dst_ref=back.at[me],
-            send_sem=send_2.at[to],
-            recv_sem=recv_2.at[me],
+            src_ref=back_stage.at[to, :, slab(h)],
+            dst_ref=back.at[me, :, slab(h)],
+            send_sem=send_2.at[h, to],
+            recv_sem=recv_2.at[h, me],
             device_id={"feat": to},
             device_id_type=MESH,
         )
 
-    def backward_send(step):
+    def backward_send(step, h):
         to = (me + distance(step, n)) % n
         for k in range(CAPACITY):
             block = jnp.minimum(target[to * CAPACITY + k], BLOCKS - 1)
-            back_stage[to, k] = mean_grad[block]
-        backward_copy(step).start()
-
-    @pl.loop(1, 1 + n // 2)
-    def _(step):
-        backward_send(step)
-
-    for c in range(0, HIDDEN_SIZE, COLS):
-        cols = slice(c, c + COLS)
-        local = lax.dot_general(
-            inputs[...],
-            pre_grad[:, cols],
-            (((0,), (0,)), ((), ())),
-            preferred_element_type=F32,
-        )
-        weight_sum[0, :, cols] = local[:FEATS]
-        weight_sum[1, :, cols] = local[FEATS:]
+            back_stage[to, k, slab(h)] = mean_grad[block, slab(h)]
+        backward_copy(step, h).start()
+
+    def weight_gradients(h):
+        rows = slice(h * PART_ROWS, (h + 1) * PART_ROWS)
+        for c in range(0, HIDDEN_SIZE, COLS):
+            cols = slice(c, c + COLS)
+            local = lax.dot_general(
+                inputs[rows, :],
+                pre_grad[rows, cols],
+                (((0,), (0,)), ((), ())),
+                preferred_element_type=F32,
+            )
+            if h == 0:
+                weight_sum[0, :, cols] = local[:FEATS]
+                weight_sum[1, :, cols] = local[FEATS:]
+            else:
+                weight_sum[0, :, cols] += local[:FEATS]
+                weight_sum[1, :, cols] += local[FEATS:]
+
+    for h in range(PARTS):
+        take_forward(h)
+        layer(h)
+
+        @pl.loop(1, 1 + n // 2 if h == PARTS - 1 else n)
+        def _(step):
+            backward_send(step, h)
+
+        weight_gradients(h)
+
     bias_row = jnp.sum(bias_sum[...], axis=0, keepdims=True)
     for c in range(chips):
         cols = slice(c * width, (c + 1) * width)
@@ -294,7 +332,7 @@
 
     @pl.loop(1 + n // 2, n)
     def _(step):
-        backward_send(step)
+        backward_send(step, PARTS - 1)
 
     def backward_link(step, owner, blocks):
         for k in range(CAPACITY):
@@ -318,14 +356,15 @@
 
     def backward_take(step):
         owner = (me - distance(step, n) + n) % n
-        pltpu.make_async_remote_copy(
-            src_ref=back_stage.at[owner],
-            dst_ref=back.at[owner],
-            send_sem=send_2.at[owner],
-            recv_sem=recv_2.at[owner],
-            device_id={"feat": owner},
-            device_id_type=MESH,
-        ).wait_recv()
+        for h in range(PARTS):
+            pltpu.make_async_remote_copy(
+                src_ref=back_stage.at[owner, :, slab(h)],
+                dst_ref=back.at[owner, :, slab(h)],
+                send_sem=send_2.at[h, owner],
+                recv_sem=recv_2.at[h, owner],
+                device_id={"feat": owner},
+                device_id_type=MESH,
+            ).wait_recv()
         backward_link(step, owner, [back[owner, k] for k in range(CAPACITY)])
 
     @pl.loop(1, 1 + n // 2)
@@ -364,8 +403,8 @@
 
     mine = own_half(swap_send[:FEATS])
     theirs = own_half(swap_recv[:FEATS])
-    self_out[...] = jnp.where(core == 0, mine, theirs)
-    neigh_out[...] = jnp.where(core == 0, theirs, mine)
+    self_out[...] = jnp.where(core == 0, mine, theirs).T
+    neigh_out[...] = jnp.where(core == 0, theirs, mine).T
     bias_out[...] = own_half(jnp.sum(swap_send[FEATS:], axis=0, keepdims=True))
 
     swap_copy.wait_send()
@@ -377,8 +416,14 @@
 
     @pl.loop(1, n)
     def _(step):
-        forward_copy(step).wait_send()
-        backward_copy(step).wait_send()
+        for h in range(PARTS):
+            forward_copy(step, h).wait_send()
+            backward_copy(step, h).wait_send()
+
+
+def hand_on(*refs):
+    for i in range(4):
+        refs[4 + i][...] = refs[i][...]
 
 
 def local(
@@ -405,14 +450,14 @@
         functools.partial(kernel, n),
         out_shape=(
             jax.ShapeDtypeStruct((BLOCKS,) + block, BF16),
-            jax.ShapeDtypeStruct((FEATS, width // 2), F32),
-            jax.ShapeDtypeStruct((FEATS, width // 2), F32),
+            jax.ShapeDtypeStruct((width // 2, FEATS), F32),
+            jax.ShapeDtypeStruct((width // 2, FEATS), F32),
             jax.ShapeDtypeStruct((1, width // 2), F32),
         ),
         in_specs=[vmem, vmem, smem, smem, vmem, vmem, vmem, pl.BlockSpec(memory_space=pl.ANY)],
         out_specs=(vmem, vmem, vmem, vmem),
         scratch_shapes=[
-            pltpu.VMEM((NODE_DEV, HIDDEN_SIZE), BF16),
+            pltpu.VMEM((PARTS, BLOCKS, SLAB, HIDDEN_SIZE), BF16),
             pltpu.VMEM((n, CAPACITY) + block, BF16),
             pltpu.VMEM((n, CAPACITY) + block, BF16),
             pltpu.VMEM((n, CAPACITY) + block, BF16),
@@ -436,11 +481,11 @@
             pltpu.SMEM((BLOCKS + 1,), jnp.int32),
             pltpu.SMEM((slots,), jnp.int32),
             pltpu.SMEM((BLOCKS + 1,), jnp.int32),
-            dma,
-            dma((n,)),
-            dma((n,)),
-            dma((n,)),
-            dma((n,)),
+            dma((PARTS,)),
+            dma((PARTS, n)),
+            dma((PARTS, n)),
+            dma((PARTS, n)),
+            dma((PARTS, n)),
             dma((2,)),
             dma((chips,)),
             dma((chips,)),
@@ -458,12 +503,20 @@
         self_weight,
         neigh_weight,
         hidden_bias.reshape(1, HIDDEN_SIZE),
-        out_grad,
+        out_grad.reshape(BLOCKS, PARTS, SLAB, HIDDEN_SIZE),
     )
+    results = (feat_grad, self_grad, neigh_grad, bias_grad)
+    feat_grad, self_grad, neigh_grad, bias_grad = pl.pallas_call(
+        hand_on,
+        out_shape=tuple(jax.ShapeDtypeStruct(r.shape, r.dtype) for r in results),
+        in_specs=[vmem] * 4,
+        out_specs=(vmem,) * 4,
+        cost_estimate=pl.CostEstimate(flops=0, bytes_accessed=2**20, transcendentals=0),
+    )(*results)
     return (
         feat_grad.reshape(NODE_DEV, FEATS),
-        self_grad,
-        neigh_grad,
+        self_grad.T,
+        neigh_grad.T,
         bias_grad.reshape(width // 2),
     )
 

time: 75.9 us -> 65 us (0.86)
  local copies, waits for them, and re-layouts: 6.11 us -> 0 us
  Pallas kernels: 68.9 us -> 63.5 us
    pallas_call x1, Pallas kernels: 68.9 us -> 61.6 us  [local(): pl.pallas_call(functools.partial(kernel, n), out_shape=(jax.ShapeDtypeStr...]
    unnamed x4 -> x0, local copies, waits for them, and re-layouts: 6.11 us -> none
    pallas_call x0 -> x1, Pallas kernels: none -> 1.9 us  [local(): pl.pallas_call(hand_on, out_shape=tuple((jax.ShapeDtypeStruct(r.shape, r....]
where the time goes in v2:
time: 65 us; the launch traced here: 64.1 us
  Pallas kernels  63.5 us (98%)
    pallas_call x1, Pallas kernels, local(): pl.pallas_call(functools.partial(kernel, n), out_shape=(jax.ShapeDtypeStr...  61.6 us
    pallas_call x1, Pallas kernels, local(): pl.pallas_call(hand_on, out_shape=tuple((jax.ShapeDtypeStruct(r.shape, r....  1.9 us

profile of v2, /device:TPU:0, one launch (start us, length us, event | category | flops | bytes accessed | tf_op | source)
XLA Modules:
  0.0 64.1 jit_solution(12513646351514576736)
XLA Ops:
  0.6 61.6 %shard_map.111 = (bf16[16,128,128]{2,1,0:T(8,128)(2,1)}, f32[64,128]{1,0:T(8,128)}, f32[64,128]{1,0:T(8,128)}, f32[1,64]{1,0:T(1,128)}) custom-call(bf16[16,128,128]{2,1,0:T(8,128)(2,1)} %bitcast.8, bf16[32,128,128]{2,1,0:T(8,128)(2,1)} %tiles.1, s32[32]{0:T(128)} %source.1, s32[32]{0:T(128)} %target.1, bf16[128,1024]{1,0:T(8,128)(2,1)} %self_w.1, ...), custom_call_target="tpu_custom_call" | custom-call | flops 3489660928 | bytes 8388608 | tf_op jit(solution)/shard_map/pallas_call | solution.py:449
  62.2 1.9 %shard_map.112 = (bf16[16,128,128]{2,1,0:T(8,128)(2,1)}, f32[64,128]{1,0:T(8,128)}, f32[64,128]{1,0:T(8,128)}, f32[1,64]{1,0:T(1,128)}) custom-call(bf16[16,128,128]{2,1,0:T(8,128)(2,1)} %get-tuple-element.12.refs_0_, f32[64,128]{1,0:T(8,128)} %get-tuple-element.13.refs_1_, f32[64,128]{1,0:T(8,128)} %get-tuple-element.14.refs_2_, ...), custom_call_target="tpu_custom_call" | custom-call | bytes 1048576 | tf_op jit(solution)/shard_map/pallas_call | solution.py:509

commit v3 on v2

--- a/solution.py
+++ b/solution.py
@@ -18,6 +18,7 @@
 BIAS_ROWS = 16
 EARLY = 3
 PARTS = 2
+AHEAD = (4, 5, 6)
 SLAB = TILE // PARTS
 PART_ROWS = NODE_DEV // PARTS
 MESH = pl.DeviceIdType.MESH
@@ -70,6 +71,8 @@
     pair_send,
     pair_recv,
     share_send,
+    side_recv,
+    layer_send,
     share_recv,
     swap_send,
     swap_recv,
@@ -83,6 +86,7 @@
     send_2,
     recv_2,
     pair_sems,
+    side_sems,
     send_b,
     recv_b,
     swap_sems,
@@ -95,6 +99,10 @@
     core = me % 2
     chip = me // 2
     sibling = chip * 2 + 1 - core
+    layers = chips // 2
+    side = chip % 2
+    layer_id = chip // 2
+    beside = (layer_id * 2 + 1 - side) * 2 + core
 
     barrier = pltpu.get_barrier_semaphore()
 
@@ -266,6 +274,11 @@
             back_stage[to, k, slab(h)] = mean_grad[block, slab(h)]
         backward_copy(step, h).start()
 
+    def last_sends(first, end):
+        @pl.loop(first, end)
+        def _(step):
+            backward_send(step, PARTS - 1)
+
     def weight_gradients(h):
         rows = slice(h * PART_ROWS, (h + 1) * PART_ROWS)
         for c in range(0, HIDDEN_SIZE, COLS):
@@ -287,7 +300,7 @@
         take_forward(h)
         layer(h)
 
-        @pl.loop(1, 1 + n // 2 if h == PARTS - 1 else n)
+        @pl.loop(1, 1 + n * AHEAD[0] // 8 if h == PARTS - 1 else n)
         def _(step):
             backward_send(step, h)
 
@@ -307,32 +320,47 @@
         device_id_type=MESH,
     )
     pair_copy.start()
+    last_sends(1 + n * AHEAD[0] // 8, 1 + n * AHEAD[1] // 8)
     pair_copy.wait_recv()
     for c in range(chips):
         cols = slice(c * width, (c + 1) * width)
-        share_send[c, :FEATS] = (
+        share_send[c % 2, c // 2, :FEATS] = (
             weight_sum[core, :, cols] + pair_recv[c, :FEATS].astype(F32)
         ).astype(BF16)
         other = jnp.sum(pair_recv[c, FEATS:].astype(F32), axis=0, keepdims=True)
-        share_send[c, FEATS:] = split_bias(bias_row[:, cols] + other)
+        share_send[c % 2, c // 2, FEATS:] = split_bias(bias_row[:, cols] + other)
+
+    side_copy = pltpu.make_async_remote_copy(
+        src_ref=share_send.at[1 - side],
+        dst_ref=side_recv,
+        send_sem=side_sems.at[0],
+        recv_sem=side_sems.at[1],
+        device_id={"feat": beside},
+        device_id_type=MESH,
+    )
+    side_copy.start()
+    last_sends(1 + n * AHEAD[1] // 8, 1 + n * AHEAD[2] // 8)
+    side_copy.wait_recv()
+    for c in range(layers):
+        summed = share_send[side, c].astype(F32) + side_recv[c].astype(F32)
+        layer_send[c, :FEATS] = summed[:FEATS].astype(BF16)
+        layer_send[c, FEATS:] = split_bias(jnp.sum(summed[FEATS:], axis=0, keepdims=True))
 
     def share_copy(to, slot):
         return pltpu.make_async_remote_copy(
-            src_ref=share_send.at[to],
+            src_ref=layer_send.at[to],
             dst_ref=share_recv.at[slot],
             send_sem=send_b.at[to],
             recv_sem=recv_b.at[slot],
-            device_id={"feat": to * 2 + core},
+            device_id={"feat": (to * 2 + side) * 2 + core},
             device_id_type=MESH,
         )
 
-    @pl.loop(1, chips)
+    @pl.loop(1, layers)
     def _(d):
-        share_copy((chip + d) % chips, chip).start()
-
-    @pl.loop(1 + n // 2, n)
-    def _(step):
-        backward_send(step, PARTS - 1)
+        share_copy((layer_id + d) % layers, layer_id).start()
+
+    last_sends(1 + n * AHEAD[2] // 8, n)
 
     def backward_link(step, owner, blocks):
         for k in range(CAPACITY):
@@ -371,11 +399,11 @@
     def _(step):
         backward_take(step)
 
-    swap_send[...] = share_send[chip].astype(F32)
-
-    @pl.loop(1, chips)
+    swap_send[...] = layer_send[layer_id].astype(F32)
+
+    @pl.loop(1, layers)
     def _(d):
-        other = (chip + d) % chips
+        other = (layer_id + d) % layers
         share_copy(other, other).wait_recv()
         swap_send[...] += share_recv[other].astype(F32)
 
@@ -409,10 +437,11 @@
 
     swap_copy.wait_send()
     pair_copy.wait_send()
-
-    @pl.loop(1, chips)
+    side_copy.wait_send()
+
+    @pl.loop(1, layers)
     def _(d):
-        share_copy((chip + d) % chips, chip).wait_send()
+        share_copy((layer_id + d) % layers, layer_id).wait_send()
 
     @pl.loop(1, n)
     def _(step):
@@ -473,8 +502,10 @@
             pltpu.VMEM((8, HIDDEN_SIZE), F32),
             pltpu.VMEM((chips, share_rows, width), BF16),
             pltpu.VMEM((chips, share_rows, width), BF16),
-            pltpu.VMEM((chips, share_rows, width), BF16),
-            pltpu.VMEM((chips, share_rows, width), BF16),
+            pltpu.VMEM((2, chips // 2, share_rows, width), BF16),
+            pltpu.VMEM((chips // 2, share_rows, width), BF16),
+            pltpu.VMEM((chips // 2, share_rows, width), BF16),
+            pltpu.VMEM((chips // 2, share_rows, width), BF16),
             pltpu.VMEM((share_rows, width), F32),
             pltpu.VMEM((share_rows, width), F32),
             pltpu.SMEM((slots,), jnp.int32),
@@ -487,8 +518,9 @@
             dma((PARTS, n)),
             dma((PARTS, n)),
             dma((2,)),
-            dma((chips,)),
-            dma((chips,)),
+            dma((2,)),
+            dma((chips // 2,)),
+            dma((chips // 2,)),
             dma((2,)),
         ],
         compiler_params=pltpu.CompilerParams(

time: 65 us -> 62.9 us (0.968); the launches traced: 64.1 us -> 62.8 us
  Pallas kernels: 63.5 us -> 62.1 us
    pallas_call x1, Pallas kernels: 61.6 us -> 60.2 us  [local(): pl.pallas_call(functools.partial(kernel, n), out_shape=(jax.ShapeDtypeStr...]
where the time goes in v3:
time: 62.9 us; the launch traced here: 62.8 us
  Pallas kernels  62.1 us (99%)
  between operations  0.64 us (1%)
    pallas_call x1, Pallas kernels, local(): pl.pallas_call(functools.partial(kernel, n), out_shape=(jax.ShapeDtypeStr...  60.2 us
    pallas_call x1, Pallas kernels, local(): pl.pallas_call(hand_on, out_shape=tuple((jax.ShapeDtypeStruct(r.shape, r....  1.9 us

profile of v3, /device:TPU:0, one launch (start us, length us, event | category | flops | bytes accessed | tf_op | source)
XLA Modules:
  0.0 62.8 jit_solution(7238956919415755106)
XLA Ops:
  0.6 60.2 %shard_map.111 = (bf16[16,128,128]{2,1,0:T(8,128)(2,1)}, f32[64,128]{1,0:T(8,128)}, f32[64,128]{1,0:T(8,128)}, f32[1,64]{1,0:T(1,128)}) custom-call(bf16[16,128,128]{2,1,0:T(8,128)(2,1)} %bitcast.8, bf16[32,128,128]{2,1,0:T(8,128)(2,1)} %tiles.1, s32[32]{0:T(128)} %source.1, s32[32]{0:T(128)} %target.1, bf16[128,1024]{1,0:T(8,128)(2,1)} %self_w.1, ...), custom_call_target="tpu_custom_call" | custom-call | flops 3489660928 | bytes 8388608 | tf_op jit(solution)/shard_map/pallas_call | solution.py:478
  60.9 1.9 %shard_map.112 = (bf16[16,128,128]{2,1,0:T(8,128)(2,1)}, f32[64,128]{1,0:T(8,128)}, f32[64,128]{1,0:T(8,128)}, f32[1,64]{1,0:T(1,128)}) custom-call(bf16[16,128,128]{2,1,0:T(8,128)(2,1)} %get-tuple-element.12.refs_0_, f32[64,128]{1,0:T(8,128)} %get-tuple-element.13.refs_1_, f32[64,128]{1,0:T(8,128)} %get-tuple-element.14.refs_2_, ...), custom_call_target="tpu_custom_call" | custom-call | bytes 1048576 | tf_op jit(solution)/shard_map/pallas_call | solution.py:541
